TPU v7x, 32 devices: a whole 2x2x4 slice. The times are simulated.
32 devices in a mesh: req: 4 (over x, core), blk: 8 (over z, y).
Axes of the slice: x: 2, y: 2, z: 4, core: 2. Of those that a mesh axis runs over, the one named last changes fastest.
Arguments:
- queries: bfloat16 [4, 8, 512, 512], P('req', 'blk'), may hold values from -6 to 6
- keys: bfloat16 [4, 8, 512, 256], P('req', 'blk'), may hold values from -25 to 25
- values: bfloat16 [4, 8, 512, 256], P('req', 'blk'), may hold values from -6 to 6
- block_map: int32 [4, 2, 2], P('req'), may hold values from 0 to 3, as said below
- lengths: int32 [4], P('req'), may hold values from 256 to 1024
- group_of_prompt: int32 [4], replicated, may hold values from 0 to 3, each once
- decode_rank: int32 [4, 8], P('req'), may hold values from 0 to 7, as said below
Outputs:
- attended: bfloat16 [4, 8, 512, 512], P('req', 'blk')
- cache: bfloat16 [4, 1024, 2048], P('req', 'blk')
Inputs may be any that keep to these rules, and one draw needn't show every extreme that they name: In each group, block_map[g] holds each of 0 to 3 once, and the two halves of each slot hold blocks b and 3 - b, in either order. `decode_rank`: each group's row holds each of 0 to 7 once.
All inputs are finite; a program needn't handle non-finite values.
Results may differ from a plain program's by a relative error of at most 0.0098.
Values may be sent and summed in bfloat16 or wider, within the bound.
No kernel may reach another device: no remote copies, remote signals or barrier semaphores. Data moves between devices by JAX's collectives and lax.ppermute only.
A program may use at most 64 MiB of HBM per device.

v0:
```python
import math

import jax
import jax.numpy as jnp
from jax import lax
from jax.sharding import PartitionSpec as P

QUERY_HEADS = 16
KEY_VALUE_HEADS = 8
HEAD_SIZE = 128
HEAD_DIVISIONS = 4
Q_DEV = 4
KV_DEV = 2


cap_value = 50.0
query_scale = 1.0 / 12.0
rope_base = 10000.0


def shifted(shard, axis, by):
    peers = lax.axis_size(axis)
    return lax.ppermute(shard, axis, [(i, (i + by) % peers) for i in range(peers)])


def apply_rotary(row_block, token_position, head_count):
    row_count = row_block.shape[0]
    head_width = row_block.shape[1] // head_count
    half_width = head_width // 2
    shaped = row_block.astype(jnp.float32).reshape(row_count, head_count, head_width)
    frequency = jnp.exp(
        -math.log(rope_base) * (2.0 * jnp.arange(half_width, dtype=jnp.float32)) / head_width
    )
    angles = token_position.astype(jnp.float32)[:, None] * frequency[None, :]
    cosine = jnp.cos(angles)[:, None, :]
    sine_part = jnp.sin(angles)[:, None, :]
    front_half = shaped[:, :, :half_width]
    second = shaped[:, :, half_width:]
    turned = jnp.concatenate(
        [front_half * cosine - second * sine_part, second * cosine + front_half * sine_part], axis=2
    )
    return turned.reshape(row_count, head_count * head_width)


def slot_positions(table, slot, block_len):
    slot_ids = jnp.arange(table.shape[0], dtype=jnp.int32)
    chosen = jnp.sum(jnp.where((slot_ids == slot)[:, None], table, 0), axis=0)
    return chosen[:, None] * block_len + jnp.arange(block_len, dtype=jnp.int32)[None, :]


def forward_step(buffer):
    return shifted(buffer, "blk", HEAD_DIVISIONS)


def on_device(queries, keys, values, block_map, lengths, group_of_prompt, decode_rank):
    token_rows = queries.shape[2]
    block_len = token_rows // 2
    rank_count = lax.axis_size("blk")
    cache_slot_count = rank_count // HEAD_DIVISIONS
    member = lax.axis_index("blk")
    own_slot = member // HEAD_DIVISIONS
    group_id = lax.axis_index("req")
    group_portion = QUERY_HEADS // KEY_VALUE_HEADS
    kv_dev_width = KV_DEV * HEAD_SIZE
    all_lengths = lax.all_gather(lengths, "req", axis=0, tiled=True)
    length = jnp.sum(jnp.where(group_of_prompt == group_id, all_lengths, 0))
    table = block_map[0]
    own_pos = slot_positions(table, own_slot, block_len)
    flat_pos = own_pos.reshape(-1)
    query_rot = (apply_rotary(queries[0, 0], flat_pos, Q_DEV) * query_scale).astype(jnp.bfloat16)
    rotated_key = apply_rotary(keys[0, 0], flat_pos, KV_DEV).astype(jnp.bfloat16)
    value_row_list = values[0, 0]
    query_halves = query_rot.reshape(2, block_len, KV_DEV, group_portion, HEAD_SIZE)

    def attend_tile(numerator, denominator, portion, key_sub, value_sub, key_pos):
        scores = jnp.einsum(
            "qkgd,nkd->kgqn", query_halves[portion], key_sub, preferred_element_type=jnp.float32
        )
        capped = cap_value * jnp.tanh(scores / cap_value)
        allowed = key_pos[None, :] <= own_pos[portion][:, None]
        expo_vals = jnp.where(allowed[None, None], jnp.exp(capped), 0.0)
        weight = expo_vals.astype(jnp.bfloat16)
        numerator = numerator + jnp.einsum(
            "kgqn,nkd->qkgd", weight, value_sub, preferred_element_type=jnp.float32
        )
        denominator = denominator + jnp.sum(expo_vals, axis=3)
        return (numerator, denominator)

    def absorb(totals, packet, slot):
        numerator, denominator = totals
        key_pos = slot_positions(table, slot, block_len)
        key_blocks = packet[0].reshape(2, block_len, KV_DEV, HEAD_SIZE)
        value_blocks = packet[1].reshape(2, block_len, KV_DEV, HEAD_SIZE)
        new_numer = []
        new_denom = []
        for portion in range(2):
            result_pair = (numerator[portion], denominator[portion])
            for half in range(2):
                result_pair = attend_tile(
                    result_pair[0],
                    result_pair[1],
                    portion,
                    key_blocks[half],
                    value_blocks[half],
                    key_pos[half],
                )
            new_numer.append(result_pair[0])
            new_denom.append(result_pair[1])
        return (jnp.stack(new_numer), jnp.stack(new_denom))

    packet = jnp.stack([rotated_key, value_row_list])
    start_numer = jnp.zeros((2, block_len, KV_DEV, group_portion, HEAD_SIZE), jnp.float32)
    start_denom = jnp.zeros((2, KV_DEV, group_portion, block_len), jnp.float32)
    numerator, denominator = absorb((start_numer, start_denom), packet, own_slot)

    def step_single(turn, carry):
        numer_now, denom_now, buffer = carry
        buffer = forward_step(buffer)
        numer_now, denom_now = absorb(
            (numer_now, denom_now), buffer, (own_slot - turn) % cache_slot_count
        )
        return (numer_now, denom_now, buffer)

    numerator, denominator, _ = lax.fori_loop(
        1, cache_slot_count, step_single, (numerator, denominator, packet)
    )
    safe_denom = jnp.where(denominator > 0.0, denominator, 1.0)
    output = numerator / jnp.transpose(safe_denom, (0, 3, 1, 2))[..., None]
    output = output.reshape(token_rows, Q_DEV * HEAD_SIZE)
    live = flat_pos < length
    attended = jnp.where(live[:, None], output, 0.0).astype(jnp.bfloat16)
    joined = jnp.concatenate([rotated_key, value_row_list], axis=1)
    kept_rows = jnp.where(live[:, None], joined, jnp.zeros_like(joined))
    rank_portion = block_len // rank_count
    shaped = kept_rows.reshape(2, rank_portion, rank_count, 2 * kv_dev_width)
    rank_of = decode_rank[0]
    rank_ids = jnp.arange(rank_count, dtype=jnp.int32)
    inverse = jnp.sum(
        jnp.where(rank_of[None, :] == rank_ids[:, None], rank_ids[None, :], 0), axis=1
    )
    outgoing = jnp.take(shaped, inverse, axis=2)
    arrived = lax.all_to_all(outgoing, "blk", split_axis=2, concat_axis=2, tiled=True)
    regrouped = arrived.reshape(2, rank_portion, cache_slot_count, HEAD_DIVISIONS, 2, kv_dev_width)
    regrouped = jnp.transpose(regrouped, (2, 0, 1, 4, 3, 5)).reshape(
        cache_slot_count * 2 * rank_portion, 2 * KEY_VALUE_HEADS * HEAD_SIZE
    )
    target = (
        table.reshape(-1)[:, None] * rank_portion
        + jnp.arange(rank_portion, dtype=jnp.int32)[None, :]
    )
    cache_rows = (
        jnp.zeros((token_rows // HEAD_DIVISIONS, 2 * KEY_VALUE_HEADS * HEAD_SIZE), jnp.bfloat16)
        .at[target.reshape(-1)]
        .set(regrouped)
    )
    return (attended[None, None], cache_rows[None])


def solution(mesh):
    placed = (
        P("req", "blk", None, None),
        P("req", "blk", None, None),
        P("req", "blk", None, None),
        P("req", None, None),
        P("req"),
        P(),
        P("req", None),
    )
    return jax.shard_map(
        on_device,
        mesh=mesh,
        in_specs=placed,
        out_specs=(P("req", "blk", None, None), P("req", "blk", None)),
        check_vma=False,
    )
```

profile of v0, /device:TPU:0, one launch (start us, length us, event | category | flops | bytes accessed | tf_op | source)
XLA Modules:
  0.0 50.9 jit_solution(14735697089263910752)
XLA Ops:
  0.7 0.7 %copy-done.6 = s32[1,2,2]{2,1,0:T(2,128)S(1)} copy-done((s32[1,2,2]{2,1,0:T(2,128)S(1)}, s32[1,2,2]{2,1,0:T(2,128)}, u32[]{:S(2)}) %copy-start.6) | copy-done | bytes 40
  1.4 0.1 fusion.64
  1.6 1.1 %copy.93 = bf16[1,1,512,256]{2,3,1,0:T(8,128)(2,1)S(1)} copy(bf16[1,1,512,256]{3,2,1,0:T(8,128)(2,1)} %param.8) | data formatting | bytes 524288 | tf_op args[1]
  2.7 0.2 copy.170
  2.9 0.2 copy.171
  3.1 1.0 %multiply_cosine_fusion = (f32[512,64]{1,0:T(8,128)S(1)}, f32[512,64]{1,0:T(8,128)S(1)}) fusion(f32[64]{0:T(128)S(1)} %multiply_exponential_fusion, f32[512]{0:T(512)S(1)} %bitcast.216), kind=kLoop, calls=%fused_computation.87 | loop fusion | flops 32768 | bytes 264448 | tf_op jit(solution)/shard_map/cos | solution.py:35
  4.1 0.1 multiply_subtract_fusion.1
  4.3 0.1 maximum_convert_fusion
  4.4 0.1 copy.104
  4.6 0.8 %copy-done = bf16[1,1,512,256]{3,2,1,0:T(8,128)(2,1)S(1)} copy-done((bf16[1,1,512,256]{3,2,1,0:T(8,128)(2,1)S(1)}, bf16[1,1,512,256]{3,2,1,0:T(8,128)(2,1)}, u32[]{:S(2)}) %copy-start) | copy-done | bytes 262168
  5.4 0.1 copy.98
  5.5 0.8 %pad_maximum_fusion = bf16[2,512,256]{1,2,0:T(8,128)(2,1)} fusion(bf16[1,512,256]{1,2,0:T(8,128)(2,1)S(1)} %bitcast.189, bf16[1,512,256]{1,2,0:T(8,128)(2,1)S(1)} %bitcast.200), kind=kLoop, calls=%fused_computation.71 | loop fusion | flops 262144 | bytes 1048576 | tf_op jit(solution)/shard_map/stack | solution.py:111
  6.4 4.0 %collective-permute-start = (bf16[2,512,256]{1,2,0:T(8,128)(2,1)}, bf16[2,512,256]{1,2,0:T(8,128)(2,1)}, u32[]{:S(2)}, u32[]{:S(2)}) collective-permute-start(bf16[2,512,256]{1,2,0:T(8,128)(2,1)} %pad_maximum_fusion), channel_id=1, source_target_pairs={{0,4},{1,5},{2,6},{3,7},{4,0},{5,1},{6,2},{7,3},{8,12},{9,13},{10,... | collective-permute-start | bytes 1572872 | tf_op jit(solution)/shard_map/while/body/eval_jaxpr/ppermute | solution.py:23
  10.4 0.7 %copy-done.9 = s32[1,8]{1,0:T(1,128)S(1)} copy-done((s32[1,8]{1,0:T(1,128)S(1)}, s32[1,8]{1,0:T(1,128)}, u32[]{:S(2)}) %copy-start.9) | copy-done | bytes 56
  11.1 0.1 select_reduce_fusion
  11.9 0.6 %dynamic-slice = u32[1]{0:T(128)} dynamic-slice(u32[32]{0:T(128)S(1)} %copy-done.10, u32[]{:T(128)S(6)} %add.278), dynamic_slice_sizes={1} | dynamic-slice | bytes 12
  12.5 0.8 %dynamic-update-slice = s32[4]{0:T(128)S(1)} dynamic-update-slice(s32[4]{0:T(128)S(1)} %broadcast.360, s32[1]{0:T(128)S(6)} %copy.180, u32[]{:T(128)} %bitcast.1) | dynamic-update-slice | bytes 12
  13.2 0.3 copy.123
  13.5 4.9 %all-reduce = s32[4]{0:T(128)S(1)} all-reduce(s32[4]{0:T(128)S(1)} %dynamic-update-slice), channel_id=1, replica_groups=mesh['req'=4,'blk'=8] {'req'}, use_global_device_ids=true, to_apply=%add | all-reduce | flops 4 | bytes 32
  18.4 0.2 convert_element_type.103
  18.7 0.6 %copy-done.8 = s32[4]{0:T(128)S(1)} copy-done((s32[4]{0:T(128)S(1)}, s32[4]{0:T(128)}, u32[]{:S(2)}) %copy-start.8) | copy-done | bytes 40
  19.3 0.6 %fusion.65 = s32[]{:T(128)} fusion(s32[4]{0:T(128)S(1)} %all-reduce, s32[4]{0:T(128)S(1)} %copy-done.8, s32[]{:T(128)S(6)} %axis_index.25), kind=kLoop, calls=%fused_computation.122 | loop fusion | flops 11 | bytes 40 | tf_op jit(solution)/shard_map/reduce_sum | solution.py:66
  19.9 0.7 %add_compare_fusion = pred[2,32,8]{1,2,0:T(8,128)(4,1)S(1)} fusion(s32[]{:T(128)} %fusion.65, s32[2]{0:T(128)S(1)} %broadcast_multiply_fusion.2), kind=kLoop, calls=%fused_computation.102 | loop fusion | flops 2048 | bytes 524 | tf_op jit(solution)/shard_map/lt | solution.py:130
  20.7 0.2 maximum_select_fusion
  20.9 0.6 %gather_fusion = bf16[8,2,32,512]{3,2,1,0:T(8,128)(2,1)S(1)} fusion(bf16[2,32,8,512]{3,1,2,0:T(8,128)(2,1)S(1)} %maximum_select_fusion, s32[1024]{0:T(1024)S(1)} %pad_clamp_fusion), kind=kCustom, calls=%fused_computation | custom fusion | bytes 1048608 | tf_op jit(solution)/shard_map/jit(_take)/gather | solution.py:141
  21.5 0.9 %select_bitcast_fusion = bf16[2,32,8,512]{3,1,0,2:T(8,128)(2,1)} fusion(bf16[8,2,32,512]{3,2,1,0:T(8,128)(2,1)S(1)} %gather_fusion, pred[8]{0:T(512)(128)(4,1)S(1)} %compare_and_fusion), kind=kLoop, calls=%fused_computation.73 | loop fusion | flops 262144 | bytes 1048584 | tf_op jit(solution)/shard_map/jit(_take)/select_n | solution.py:141
  22.4 3.8 %all-to-all-start = ((bf16[2,32,8,512]{3,1,0,2:T(8,128)(2,1)}), bf16[2,32,8,512]{3,1,0,2:T(8,128)(2,1)S(1)}, u32[]{:S(2)}, u32[]{:S(2)}) async-start(bf16[2,32,8,512]{3,1,0,2:T(8,128)(2,1)} %select_bitcast_fusion), calls=%async_computation | async-start | bytes 1048576 | tf_op jit(solution)/shard_map/all_to_all | solution.py:142
  26.2 1.3 %fusion.62 = pred[2,256]{1,0:T(4,128)(4,1)} fusion(s32[2]{0:T(128)S(1)} %broadcast_multiply_fusion.2, s32[]{:T(128)} %fusion.65), kind=kLoop, calls=%fused_computation.117 | loop fusion | flops 1024 | bytes 524 | tf_op jit(solution)/shard_map/lt | solution.py:130
  27.6 0.6 %broadcast_multiply_fusion = s32[1,2,2]{2,1,0:T(2,128)} fusion(s32[1,2,2]{2,1,0:T(2,128)S(1)} %copy-done.6), kind=kLoop, calls=%fused_computation.125 | loop fusion | flops 4 | bytes 32 | tf_op jit(solution)/shard_map/mul | solution.py:148
  28.1 0.3 reshape.576
  28.5 0.6 %fusion.68 = (f32[512,4,64]{2,1,0:T(4,128)S(1)}, f32[512,4,64]{2,1,0:T(4,128)S(1)}) fusion(f32[512,4,128]{2,1,0:T(4,128)S(1)} %reshape.576), kind=kLoop, calls=%fused_computation.131 | loop fusion | bytes 2097152 | tf_op jit(solution)/shard_map/slice | solution.py:37
  29.1 0.2 multiply_subtract_fusion
  29.3 0.3 fusion.48
  29.8 1.0 %broadcast_compare_fusion.5 = (pred[256,256]{0,1:T(8,128)(4,1)}, pred[256,256]{0,1:T(8,128)(4,1)}, pred[256,256]{0,1:T(8,128)(4,1)S(1)}, pred[256,256]{0,1:T(8,1...) fusion(s32[256]{0:T(256)S(1)} %bitcast.214, ...), kind=kLoop, calls=%fused_computation.97 | loop fusion | flops 524288 | bytes 528384 | tf_op jit(solution)/shard_map/while/body/eval_jaxpr/le | solution.py:80
  30.8 0.5 fusion.82
  31.3 0.5 fusion.81
  31.8 0.5 fusion.78
  32.2 0.5 fusion.77
  32.7 0.7 %mul.188 = s32[4]{0:T(128)S(1)} reshape(s32[1,2,2]{2,1,0:T(2,128)} %broadcast_multiply_fusion) | data formatting | bytes 32 | tf_op jit(solution)/shard_map/mul | solution.py:148
  33.6 0.1 add.266
  33.6 0.3 fusion.57
  34.0 0.3 fusion.47
  34.4 0.6 %copy-done.7 = pred[2,256]{1,0:T(4,128)(4,1)S(1)} copy-done((pred[2,256]{1,0:T(4,128)(4,1)S(1)}, pred[2,256]{1,0:T(4,128)(4,1)}, u32[]{:S(2)}) %copy-start.7) | copy-done | bytes 536
  35.0 0.3 fusion.52
  35.4 0.3 fusion.46
  35.8 4.6 %collective-permute-done = bf16[2,512,256]{1,2,0:T(8,128)(2,1)} collective-permute-done((bf16[2,512,256]{1,2,0:T(8,128)(2,1)}, bf16[2,512,256]{1,2,0:T(8,128)(2,1)}, u32[]{:S(2)}, u32[]{:S(2)}) %collective-permute-start) | collective-permute-done | bytes 524320 | tf_op jit(solution)/shard_map/while/body/eval_jaxpr/ppermute | solution.py:23
  40.4 1.1 %fusion.70 = (bf16[1,256,256]{1,2,0:T(8,128)(2,1)S(1)}, bf16[1,256,256]{1,2,0:T(8,128)(2,1)S(1)}, bf16[1,256,256]{1,2,0:T(8,128)(2,1)S(1)}, bf16[1,256,256]{1,2,0:T(8,128)(2,1)S(1)}) fusion(bf16[2,512,256]{1,2,0:T(8,128)(2,1)} %collective-permute-done), kind=kLoop, calls=%fused_computation.133 | loop fusion | bytes 1048576 | tf_op jit(solution)/shard_map/while/body/eval_jaxpr/slice | solution.py:103
  41.5 0.5 %fusion.80 = (f32[2,2,256]{2,1,0:T(2,128)S(1)}, bf16[2,2,256,256]{2,3,1,0:T(8,128)(2,1)S(1)}) fusion(bf16[256,2,128,1]{0,2,3,1:T(8,128)(2,1)S(1)} %bitcast.212, bf16[256,2,2,128]{3,0,2,1:T(8,128)(2,1)S(1)} %bitcast.208, pred[256,256]{0,1:T(8,128)(4,1)S(1)} %copy-done.5), kind=kOutput, calls=%fused_computation.143 | convolution fusion | flops 68418560 | bytes 987136 | tf_op jit(solution)/shard_map/while/body/eval_jaxpr/qkgd,nkd->kgqn/dot_general | solution.py:76
  42.1 0.3 copy-done.4
  42.4 0.5 %fusion.76 = (f32[2,2,256]{2,1,0:T(2,128)S(1)}, bf16[2,2,256,256]{2,3,1,0:T(8,128)(2,1)S(1)}) fusion(bf16[256,2,128,1]{0,2,3,1:T(8,128)(2,1)S(1)} %bitcast.213, bf16[256,2,2,128]{3,0,2,1:T(8,128)(2,1)S(1)} %bitcast.204, pred[256,256]{0,1:T(8,128)(4,1)S(1)} %copy-done.4), kind=kOutput, calls=%fused_computation.139 | convolution fusion | flops 68418560 | bytes 987136 | tf_op jit(solution)/shard_map/while/body/eval_jaxpr/qkgd,nkd->kgqn/dot_general | solution.py:76
  42.9 0.5 %fusion.79 = (f32[2,2,256]{2,1,0:T(2,128)S(1)}, bf16[2,2,256,256]{2,3,1,0:T(8,128)(2,1)S(1)}) fusion(bf16[256,2,128,1]{0,2,3,1:T(8,128)(2,1)S(1)} %bitcast.210, bf16[256,2,2,128]{3,0,2,1:T(8,128)(2,1)S(1)} %bitcast.209, pred[256,256]{0,1:T(8,128)(4,1)S(1)} %get-tuple-element.61), kind=kOutput, calls=%fused_computation.142 | convolution fusion | flops 68418560 | bytes 987136 | tf_op jit(solution)/shard_map/while/body/eval_jaxpr/qkgd,nkd->kgqn/dot_general | solution.py:76
  43.4 0.5 %fusion.75 = (f32[2,2,256]{2,1,0:T(2,128)S(1)}, bf16[2,2,256,256]{2,3,1,0:T(8,128)(2,1)S(1)}) fusion(bf16[256,2,128,1]{0,2,3,1:T(8,128)(2,1)S(1)} %bitcast.211, bf16[256,2,2,128]{3,0,2,1:T(8,128)(2,1)S(1)} %bitcast.205, pred[256,256]{0,1:T(8,128)(4,1)S(1)} %get-tuple-element.60), kind=kOutput, calls=%fused_computation.138 | convolution fusion | flops 68418560 | bytes 987136 | tf_op jit(solution)/shard_map/while/body/eval_jaxpr/qkgd,nkd->kgqn/dot_general | solution.py:76
  44.0 0.3 convolution_bitcast_fusion.2
  44.4 0.4 fusion.42
  44.7 0.3 convolution_bitcast_fusion
  45.1 0.4 fusion.45
  45.4 0.3 maximum_divide_fusion
  45.8 0.5 %copy.122 = bf16[2,256,2,2,128]{4,3,2,1,0:T(2,128)(2,1)S(1)} copy(bf16[2,256,2,2,128]{4,1,3,2,0:T(8,128)(2,1)S(1)} %maximum_divide_fusion) | data formatting | bytes 1048576 | tf_op jit(solution)/shard_map/div | solution.py:128
  46.3 0.2 div.76
  46.5 1.0 %select_convert_fusion = bf16[1,1,512,512]{3,2,1,0:T(8,128)(2,1)} fusion(bf16[1,1,512,512]{3,2,1,0:T(8,128)(2,1)S(1)} %div.76, pred[512]{0:T(512)(128)(4,1)S(1)} %lt.57), kind=kLoop, calls=%fused_computation.67 | loop fusion | flops 262144 | bytes 1049088 | tf_op jit(solution)/shard_map/convert_element_type | solution.py:131
  47.5 0.1 reshape.610
  47.7 0.7 %copy.127 = bf16[2,2,32,2,4,256]{5,4,3,2,1,0:T(4,128)(2,1)S(1)} copy(bf16[2,2,32,2,4,256]{5,3,2,1,4,0:T(2,128)(2,1)S(1)} %bitcast.190) | data formatting | bytes 1048576 | tf_op jit(solution)/shard_map/transpose | solution.py:144
  48.3 0.4 reshape.589
  48.7 2.1 %scatter_custom_fusion = bf16[128,2048]{1,0:T(8,128)(2,1)} fusion(s32[128]{0:T(128)S(1)} %fusion.66, bf16[128,2048]{1,0:T(8,128)(2,1)S(1)} %reshape.589, bf16[]{:T(256)} %constant.94.clone.1), kind=kCustom, calls=%fused_computation.88 | custom fusion | bytes 524290 | tf_op jit(solution)/shard_map/scatter | solution.py:154
  (41 shorter events, 0.6 us)
Async XLA Ops:
  0.7 0.7 %copy-start.6 = (s32[1,2,2]{2,1,0:T(2,128)S(1)}, s32[1,2,2]{2,1,0:T(2,128)}, u32[]{:S(2)}) copy-start(s32[1,2,2]{2,1,0:T(2,128)} %param.10) | copy-start | bytes 52
  4.4 1.0 %copy-start = (bf16[1,1,512,256]{3,2,1,0:T(8,128)(2,1)S(1)}, bf16[1,1,512,256]{3,2,1,0:T(8,128)(2,1)}, u32[]{:S(2)}) copy-start(bf16[1,1,512,256]{3,2,1,0:T(8,128)(2,1)} %param.9) | copy-start | bytes 786436
  6.4 34.0 %collective-permute-start = (bf16[2,512,256]{1,2,0:T(8,128)(2,1)}, bf16[2,512,256]{1,2,0:T(8,128)(2,1)}, u32[]{:S(2)}, u32[]{:S(2)}) collective-permute-start(bf16[2,512,256]{1,2,0:T(8,128)(2,1)} %pad_maximum_fusion), channel_id=1, source_target_pairs={{0,4},{1,5},{2,6},{3,7},{4,0},{5,1},{6,2},{7,3},{8,12},{9,13},{10,... | collective-permute-start | bytes 1572872 | tf_op jit(solution)/shard_map/while/body/eval_jaxpr/ppermute | solution.py:23
  10.4 0.7 %copy-start.9 = (s32[1,8]{1,0:T(1,128)S(1)}, s32[1,8]{1,0:T(1,128)}, u32[]{:S(2)}) copy-start(s32[1,8]{1,0:T(1,128)} %param.13) | copy-start | bytes 100
  11.2 0.7 %copy-start.10 = (u32[32]{0:T(128)S(1)}, u32[32]{0:T(128)}, u32[]{:S(2)}) copy-start(u32[32]{0:T(128)} %constant.108) | copy-start | bytes 388
  18.6 0.7 %copy-start.8 = (s32[4]{0:T(128)S(1)}, s32[4]{0:T(128)}, u32[]{:S(2)}) copy-start(s32[4]{0:T(128)} %param.12) | copy-start | bytes 52
  22.4 25.2 %all-to-all-start = ((bf16[2,32,8,512]{3,1,0,2:T(8,128)(2,1)}), bf16[2,32,8,512]{3,1,0,2:T(8,128)(2,1)S(1)}, u32[]{:S(2)}, u32[]{:S(2)}) async-start(bf16[2,32,8,512]{3,1,0,2:T(8,128)(2,1)} %select_bitcast_fusion), calls=%async_computation | async-start | bytes 1048576 | tf_op jit(solution)/shard_map/all_to_all | solution.py:142
  26.2 1.9 %copy-start.1 = (bf16[1,1,512,512]{3,2,1,0:T(8,128)(2,1)S(1)}, bf16[1,1,512,512]{3,2,1,0:T(8,128)(2,1)}, u32[]{:S(2)}) copy-start(bf16[1,1,512,512]{3,2,1,0:T(8,128)(2,1)} %param.7) | copy-start | bytes 1572868
  29.7 1.6 %copy-start.2 = (bf16[256,4,128]{2,0,1:T(8,128)(2,1)}, bf16[256,4,128]{2,0,1:T(8,128)(2,1)S(1)}, u32[]{:S(2)}) copy-start(bf16[256,4,128]{2,0,1:T(8,128)(2,1)S(1)} %get-tuple-element.37) | copy-start | bytes 786436
  34.3 0.7 %copy-start.7 = (pred[2,256]{1,0:T(4,128)(4,1)S(1)}, pred[2,256]{1,0:T(4,128)(4,1)}, u32[]{:S(2)}) copy-start(pred[2,256]{1,0:T(4,128)(4,1)} %fusion.62) | copy-start | bytes 1540
  35.7 5.8 %copy-start.3 = (bf16[256,4,128]{2,0,1:T(8,128)(2,1)S(1)}, bf16[256,4,128]{2,0,1:T(8,128)(2,1)}, u32[]{:S(2)}) copy-start(bf16[256,4,128]{2,0,1:T(8,128)(2,1)} %copy-done.2) | copy-start | bytes 786436
  35.8 5.7 %copy-start.5 = (pred[256,256]{0,1:T(8,128)(4,1)S(1)}, pred[256,256]{0,1:T(8,128)(4,1)}, u32[]{:S(2)}) copy-start(pred[256,256]{0,1:T(8,128)(4,1)} %get-tuple-element.55) | copy-start | bytes 196612
  41.5 0.8 %copy-start.4 = (pred[256,256]{0,1:T(8,128)(4,1)S(1)}, pred[256,256]{0,1:T(8,128)(4,1)}, u32[]{:S(2)}) copy-start(pred[256,256]{0,1:T(8,128)(4,1)} %get-tuple-element.56) | copy-start | bytes 196612
where the time goes:
time: 51.3 us; the launch traced here: 50.9 us
  local copies, waits for them, and re-layouts  15 us (29%)
  other arithmetic  9.81 us (19%)
  starting transfers between devices  7.85 us (15%)
  matrix products  6.9 us (13%)
  blocking collectives  4.94 us (10%)
  waiting for transfers between devices  4.6 us (9%)
  between operations  1.79 us (3%)
    unnamed x30, local copies, waits for them, and re-layouts  6.65 us
    unnamed x1, blocking collectives  4.94 us
    ppermute x1, waiting for transfers between devices, shifted(): lax.ppermute(shard, axis, [(i, (i + by) % peers) for i in range(peers)])  4.6 us
    dot_general x8, matrix products, attend_tile(): jnp.einsum('qkgd,nkd->kgqn', query_halves[portion], key_sub, preferred_el...  4.12 us
    ppermute x1, starting transfers between devices, shifted(): lax.ppermute(shard, axis, [(i, (i + by) % peers) for i in range(peers)])  4.04 us
    all_to_all x1, starting transfers between devices, on_device(): lax.all_to_all(outgoing, 'blk', split_axis=2, concat_axis=2, tiled=True)  3.81 us
    dot_general x8, matrix products, attend_tile(): jnp.einsum('kgqn,nkd->qkgd', weight, value_sub, preferred_element_type=jn...  2.78 us
    scatter x1, local copies, waits for them, and re-layouts, on_device(): cache_rows = jnp.zeros((token_rows // HEAD_DIVISIONS, 2 * KEY_VALUE_HEADS...  2.14 us
  transfers between devices with their start and end apart: 2, of which 1 were waited for; matrix products, arithmetic and copies ran while one was open for 40% of the time, Pallas kernels for 0%

commit v1 on v0

v1 whole, which is shorter than its diff:
```python
import math

import jax
import jax.numpy as jnp
import numpy as np
from jax import lax
from jax.experimental import pallas as pl
from jax.experimental.pallas import tpu as pltpu
from jax.sharding import PartitionSpec as P

QUERY_HEADS = 16
KEY_VALUE_HEADS = 8
HEAD_SIZE = 128
HEAD_DIVISIONS = 4
Q_DEV = 4
KV_DEV = 2
KV_WIDTH = KV_DEV * HEAD_SIZE

cap_value = 50.0
query_scale = 1.0 / 12.0
rope_base = 10000.0
VMEM_BYTES = 48 * 1024 * 1024

f32 = jnp.float32
bf16 = jnp.bfloat16
SMEM = pl.BlockSpec(memory_space=pltpu.SMEM)
VMEM = pl.BlockSpec(memory_space=pltpu.VMEM)


def shifted(shard, axis, by):
    peers = lax.axis_size(axis)
    return lax.ppermute(shard, axis, [(i, (i + by) % peers) for i in range(peers)])


def crossed(shard, axis, by):
    peers = lax.axis_size(axis)
    return lax.ppermute(shard, axis, [(i, i ^ by) for i in range(peers)])


def rotary_tables(block_len, block_count):
    half = HEAD_SIZE // 2
    frequency = np.exp(
        np.float32(-math.log(rope_base)) * (2.0 * np.arange(half, dtype=np.float32)) / HEAD_SIZE
    ).astype(np.float64)

    def table(positions):
        angles = positions.astype(np.float64)[:, None] * frequency[None, :]
        cosine, sine = np.cos(angles), np.sin(angles)
        return np.stack(
            [np.concatenate([cosine, cosine], 1), np.concatenate([-sine, sine], 1)]
        ).astype(np.float32)

    return table(np.arange(block_len)), table(np.arange(block_count) * block_len)


def block_angles(row_table, block_table, block):
    row_cos, row_sin = row_table[0], row_table[1]
    blk_cos, blk_sin = block_table[0, pl.ds(block, 1)], block_table[1, pl.ds(block, 1)]
    return row_cos * blk_cos - row_sin * blk_sin, row_sin * blk_cos + row_cos * blk_sin


def turned(head, angles):
    x = head.astype(f32)
    return x * angles[0] + pltpu.roll(x, HEAD_SIZE // 2, 1) * angles[1]


def send_index(rank_ref, slot, head_group, row_ids, residues):
    residue = row_ids % residues
    rank = jnp.zeros_like(row_ids)
    for r in range(residues):
        rank = jnp.where(residue == r, rank_ref[0, r], rank)
    ahead = (rank - HEAD_DIVISIONS * slot + residues) % residues
    return jnp.where(ahead < HEAD_DIVISIONS, ahead ^ head_group, ahead)


def order_matrix(rank_ref, slot, head_group, out_rows, rows, residues):
    row_ids = lax.broadcasted_iota(jnp.int32, (1, rows), 1)
    ahead = send_index(rank_ref, slot, head_group, row_ids, residues)
    index = ahead * (rows // residues) + row_ids // residues
    out_ids = lax.broadcasted_iota(jnp.int32, (out_rows, rows), 0)
    return jnp.where(out_ids == index, 1.0, 0.0).astype(bf16)


def dot(a, b):
    return jnp.dot(a, b, preferred_element_type=f32)


def dot_t(a, b):
    return lax.dot_general(a, b, (((1,), (1,)), ((), ())), preferred_element_type=f32)


def expo_of(scores):
    return jnp.exp(cap_value * jnp.tanh(scores * (1.0 / cap_value)))


def columns(index, width=HEAD_SIZE):
    return slice(index * width, (index + 1) * width)


def call(body, out_shape, in_specs, name, scratch=(), flops=10**8, moved=10**6):
    return pl.pallas_call(
        body,
        out_shape=out_shape,
        in_specs=in_specs,
        out_specs=jax.tree.map(lambda _: VMEM, out_shape),
        scratch_shapes=scratch,
        compiler_params=pltpu.CompilerParams(vmem_limit_bytes=VMEM_BYTES),
        cost_estimate=pl.CostEstimate(flops=flops, bytes_accessed=moved, transcendentals=0),
        name=name,
    )


def order_values(values, decode_rank, slots, member):
    rows, width = values.shape
    block_len = rows // 2
    residues = decode_rank.shape[1]
    first = block_len // slots

    def body(me_ref, rank_ref, v_ref, *outs):
        slot, head_group = me_ref[0] // HEAD_DIVISIONS, me_ref[0] % HEAD_DIVISIONS
        for turn in range(1, slots):
            order = order_matrix(
                rank_ref, (slot + turn) % slots, head_group, block_len, block_len, residues
            )
            head_ref, tail_ref = outs[2 * turn - 2], outs[2 * turn - 1]
            rest = block_len - first
            for half in range(2):
                moved = dot(order, v_ref[half * block_len : (half + 1) * block_len]).astype(bf16)
                head_ref[half * first : (half + 1) * first] = moved[:first]
                tail_ref[half * rest : (half + 1) * rest] = moved[first:]

    shapes = []
    for _ in range(1, slots):
        shapes.append(jax.ShapeDtypeStruct((2 * first, width), bf16))
        shapes.append(jax.ShapeDtypeStruct((2 * (block_len - first), width), bf16))
    return call(body, shapes, [SMEM, SMEM, VMEM], "order_values")(member, decode_rank, values)


def own_part(queries, keys, values, table, member, tables):
    rows = queries.shape[0]
    block_len = rows // 2

    def body(me_ref, map_ref, q_ref, k_ref, v_ref, row_ref, blk_ref, qr_ref, kr_ref, num_ref, den_ref):
        slot = me_ref[0] // HEAD_DIVISIONS
        num_ref[...] = jnp.zeros_like(num_ref)
        den_ref[...] = jnp.zeros_like(den_ref)
        for half in range(2):
            part = columns(half, block_len)
            angles = block_angles(row_ref, blk_ref, map_ref[0, slot, half])
            for head in range(Q_DEV):
                qr_ref[part, columns(head)] = (
                    turned(q_ref[part, columns(head)], angles) * query_scale
                ).astype(bf16)
            for head in range(KV_DEV):
                kr_ref[part, columns(head)] = turned(k_ref[part, columns(head)], angles).astype(bf16)

        def tile(half, other, diagonal):
            q_part, k_part = columns(half, block_len), columns(other, block_len)
            for head in range(Q_DEV):
                key_head = head * KV_DEV // Q_DEV
                expo = expo_of(dot_t(qr_ref[q_part, columns(head)], kr_ref[k_part, columns(key_head)]))
                if diagonal:
                    row = lax.broadcasted_iota(jnp.int32, expo.shape, 0)
                    col = lax.broadcasted_iota(jnp.int32, expo.shape, 1)
                    expo = jnp.where(col <= row, expo, 0.0)
                num_ref[q_part, columns(head)] += dot(
                    expo.astype(bf16), v_ref[k_part, columns(key_head)]
                )
                lanes = expo[:, :HEAD_SIZE]
                for j in range(1, block_len // HEAD_SIZE):
                    lanes = lanes + expo[:, columns(j)]
                den_ref[q_part, columns(head)] += lanes

        for half in range(2):
            tile(half, half, True)
            pl.when(map_ref[0, slot, 1 - half] < map_ref[0, slot, half])(
                lambda half=half: tile(half, 1 - half, False)
            )

    shapes = [
        jax.ShapeDtypeStruct(queries.shape, bf16),
        jax.ShapeDtypeStruct(keys.shape, bf16),
        jax.ShapeDtypeStruct(queries.shape, f32),
        jax.ShapeDtypeStruct(queries.shape, f32),
    ]
    return call(body, shapes, [SMEM, SMEM] + [VMEM] * 5, "own_part", flops=4 * 10**8, moved=4 * 10**6)(
        member, table, queries, keys, values, *tables
    )


def other_keys(arrived, query_rot, key_rot, values, den, table, decode_rank, member, length, tables):
    rows, width = key_rot.shape
    block_len = rows // 2
    slots = table.shape[1]
    residues = decode_rank.shape[1]
    piece = rows // residues

    def body(me_ref, map_ref, rank_ref, len_ref, q_ref, k_ref, v_ref, den_ref, row_ref, blk_ref, *rest):
        in_refs, rest = rest[: slots - 1], rest[slots - 1 :]
        w_refs, rest = rest[: slots - 1], rest[slots - 1 :]
        inv_ref, e_refs, k_scr, d_scr = rest[0], rest[1:5], rest[5], rest[6]
        slot, head_group = me_ref[0] // HEAD_DIVISIONS, me_ref[0] % HEAD_DIVISIONS
        select = order_matrix(rank_ref, slot, head_group, rows // slots, rows, residues)

        def emit(place, rotated):
            chosen = dot(select, rotated).astype(bf16)
            for m in range(HEAD_DIVISIONS):
                e_refs[m][columns(place, piece)] = chosen[columns(m, piece)]

        emit(0, k_ref[...])
        emit(slots, v_ref[...])
        d_scr[...] = den_ref[...]
        order = order_matrix(rank_ref, slot, head_group, block_len, block_len, residues)
        for turn in range(1, slots):
            source = (slot - turn + slots) % slots
            w_ref = w_refs[turn - 1]
            for half in range(2):
                part = columns(half, block_len)
                angles = block_angles(row_ref, blk_ref, map_ref[0, source, half])
                for head in range(KV_DEV):
                    k_scr[part, columns(head)] = turned(
                        in_refs[turn - 1][part, columns(head)], angles
                    ).astype(bf16)
            emit(turn, k_scr[...])
            for half in range(2):
                part = columns(half, block_len)
                k_scr[part] = dot(order, k_scr[part]).astype(bf16)

            def tile(half, other):
                q_part, k_part = columns(half, block_len), columns(other, block_len)
                for head in range(Q_DEV):
                    key_head = head * KV_DEV // Q_DEV
                    expo = expo_of(
                        dot_t(q_ref[q_part, columns(head)], k_scr[k_part, columns(key_head)])
                    )
                    w_ref[head, q_part, k_part] = expo.astype(bf16)
                    lanes = expo[:, :HEAD_SIZE]
                    for j in range(1, block_len // HEAD_SIZE):
                        lanes = lanes + expo[:, columns(j)]
                    d_scr[q_part, columns(head)] += lanes

            for half in range(2):
                for other in range(2):
                    pl.when(map_ref[0, source, other] < map_ref[0, slot, half])(
                        lambda half=half, other=other: tile(half, other)
                    )
        for half in range(2):
            part = columns(half, block_len)
            start = map_ref[0, slot, half] * block_len
            live = start + lax.broadcasted_iota(jnp.int32, (block_len, 1), 0) < len_ref[0]
            for head in range(Q_DEV):
                total = jnp.sum(d_scr[part, columns(head)], axis=1, keepdims=True)
                inv_ref[part, head : head + 1] = jnp.where(live, 1.0 / total, 0.0)

    shapes = [jax.ShapeDtypeStruct((Q_DEV, rows, rows), bf16) for _ in range(1, slots)]
    shapes.append(jax.ShapeDtypeStruct((rows, HEAD_SIZE), f32))
    shapes += [
        jax.ShapeDtypeStruct(((slots + 1) * piece, width), bf16) for _ in range(HEAD_DIVISIONS)
    ]
    scratch = [pltpu.VMEM((rows, width), bf16), pltpu.VMEM((rows, Q_DEV * HEAD_SIZE), f32)]
    outs = call(
        body,
        shapes,
        [SMEM] * 4 + [VMEM] * (5 + slots),
        "other_keys",
        scratch,
        flops=3 * 10**8,
        moved=4 * 10**6,
    )(member, table, decode_rank, length, query_rot, key_rot, values, den, *tables, *arrived)
    return outs[: slots - 1], outs[slots - 1], outs[slots:]


def cache_part(first, second, table, decode_rank, member, length, block_len):
    slots = table.shape[1]
    residues = decode_rank.shape[1]
    run = block_len // residues
    cache_rows = 2 * slots * run
    width = first[0].shape[1]

    def body(me_ref, map_ref, rank_ref, len_ref, *refs):
        f_refs, s_refs, out_ref = refs[:4], refs[4:8], refs[8]
        slot, head_group = me_ref[0] // HEAD_DIVISIONS, me_ref[0] % HEAD_DIVISIONS
        residue = 0
        for r in range(1, residues):
            residue = jnp.where(rank_ref[0, r] == me_ref[0], r, residue)
        col = lax.broadcasted_iota(jnp.int32, (1, cache_rows), 1)
        part, offset = col // run, col % run
        target = jnp.zeros_like(col)
        for turn in range(slots):
            for half in range(2):
                block = map_ref[0, (slot - turn + slots) % slots, half]
                target = jnp.where(part == 2 * turn + half, block * run + offset, target)
        target = jnp.where(target * residues + residue < len_ref[0], target, -1)
        row = lax.broadcasted_iota(jnp.int32, (cache_rows, cache_rows), 0)
        place = jnp.where(row == target, 1.0, 0.0).astype(bf16)
        for m in range(HEAD_DIVISIONS):
            column = (head_group ^ m) * width
            keys = f_refs[m][:cache_rows]
            values = jnp.concatenate([f_refs[m][cache_rows:], s_refs[m][...]], axis=0)
            out_ref[:, pl.ds(pl.multiple_of(column, HEAD_SIZE), width)] = dot(place, keys).astype(bf16)
            column = column + HEAD_DIVISIONS * width
            out_ref[:, pl.ds(pl.multiple_of(column, HEAD_SIZE), width)] = dot(place, values).astype(bf16)

    shape = jax.ShapeDtypeStruct((cache_rows, 2 * HEAD_DIVISIONS * width), bf16)
    return call(body, shape, [SMEM] * 4 + [VMEM] * 8, "cache_part")(
        member, table, decode_rank, length, *first, *second
    )


def finish(weights, heads, tails, num, inverse, table, member):
    rows = num.shape[0]
    block_len = rows // 2
    slots = table.shape[1]

    def body(me_ref, map_ref, num_ref, inv_ref, *refs):
        w_refs, h_refs, t_refs = refs[: slots - 1], refs[slots - 1 : 2 * slots - 2], refs[2 * slots - 2 : 3 * slots - 3]
        out_ref, acc = refs[-2:]
        slot = me_ref[0] // HEAD_DIVISIONS
        acc[...] = num_ref[...]
        for turn in range(1, slots):
            source = (slot - turn + slots) % slots
            h_ref, t_ref, w_ref = h_refs[turn - 1], t_refs[turn - 1], w_refs[turn - 1]
            for other in range(2):
                first, rest = h_ref.shape[0] // 2, t_ref.shape[0] // 2

                def tile(half):
                    q_part, k_part = columns(half, block_len), columns(other, block_len)
                    block = jnp.concatenate(
                        [h_ref[columns(other, first)], t_ref[columns(other, rest)]], axis=0
                    )
                    for head in range(Q_DEV):
                        key_head = head * KV_DEV // Q_DEV
                        acc[q_part, columns(head)] += dot(
                            w_ref[head, q_part, k_part], block[:, columns(key_head)]
                        )

                for half in range(2):
                    pl.when(map_ref[0, source, other] < map_ref[0, slot, half])(
                        lambda half=half: tile(half)
                    )
        for head in range(Q_DEV):
            out_ref[:, columns(head)] = (acc[:, columns(head)] * inv_ref[:, head : head + 1]).astype(bf16)

    shape = jax.ShapeDtypeStruct(num.shape, bf16)
    return call(
        body,
        shape,
        [SMEM] * 2 + [VMEM] * (2 + 3 * (slots - 1)),
        "finish",
        [pltpu.VMEM(num.shape, f32)],
        flops=3 * 10**8,
        moved=4 * 10**6,
    )(member, table, num, inverse, *weights, *heads, *tails)


def on_device(queries, keys, values, block_map, lengths, group_of_prompt, decode_rank):
    rows = queries.shape[2]
    block_len = rows // 2
    slots = block_map.shape[1]
    member = lax.axis_index("blk").reshape(1).astype(jnp.int32)
    group_id = lax.axis_index("req")
    q, k, v = queries[0, 0], keys[0, 0], values[0, 0]
    tables = rotary_tables(block_len, 2 * slots)

    key_in = [shifted(k, "blk", HEAD_DIVISIONS * turn) for turn in range(1, slots)]
    ordered = order_values(v, decode_rank, slots, member)
    heads = [shifted(ordered[2 * t - 2], "blk", HEAD_DIVISIONS * t) for t in range(1, slots)]
    tails = [shifted(ordered[2 * t - 1], "blk", HEAD_DIVISIONS * t) for t in range(1, slots)]

    all_lengths = lax.all_gather(lengths, "req", axis=0, tiled=True)
    length = jnp.sum(jnp.where(group_of_prompt == group_id, all_lengths, 0)).reshape(1)

    query_rot, key_rot, num, den = own_part(q, k, v, block_map, member, tables)
    weights, inverse, pieces = other_keys(
        key_in, query_rot, key_rot, v, den, block_map, decode_rank, member, length, tables
    )
    first = [pieces[0]] + [crossed(pieces[m], "blk", m) for m in range(1, HEAD_DIVISIONS)]

    def value_piece(m):
        parts = []
        for head in heads:
            run = head.shape[0] // 2 // HEAD_DIVISIONS
            shaped = head.reshape(2, HEAD_DIVISIONS, run, KV_WIDTH)
            parts.append(shaped[:, m].reshape(2 * run, KV_WIDTH))
        return jnp.concatenate(parts, axis=0)

    second = [value_piece(0)] + [
        crossed(value_piece(m), "blk", m) for m in range(1, HEAD_DIVISIONS)
    ]
    cache = cache_part(first, second, block_map, decode_rank, member, length, block_len)
    attended = finish(weights, heads, tails, num, inverse, block_map, member)
    return (attended[None, None], cache[None])


def solution(mesh):
    placed = (
        P("req", "blk", None, None),
        P("req", "blk", None, None),
        P("req", "blk", None, None),
        P("req", None, None),
        P("req"),
        P(),
        P("req", None),
    )
    return jax.shard_map(
        on_device,
        mesh=mesh,
        in_specs=placed,
        out_specs=(P("req", "blk", None, None), P("req", "blk", None)),
        check_vma=False,
    )
```

time: 51.3 us -> 47.8 us (0.932)
  Pallas kernels: 0 us -> 11.4 us
  starting transfers between devices: 7.85 us -> 17 us
  other arithmetic: 9.81 us -> 1.37 us
  matrix products: 6.9 us -> 0 us
  local copies, waits for them, and re-layouts: 15 us -> 10.5 us
  waiting for transfers between devices: 4.6 us -> 0.83 us
    pallas_call x0 -> x5, Pallas kernels: none -> 11.4 us  [the longest x1 3.1 us: other_keys(): call(body, shapes, [SMEM] * 4 + [VMEM] * (5 + slots), 'other_keys', scrat...]
    ppermute x0 -> x6, starting transfers between devices: none -> 9.89 us  [crossed(): return lax.ppermute(shard, axis, [(i, i ^ by) for i in range(peers)])]
    dot_general x16 -> x0, matrix products: 6.9 us -> none  [the longest x8 4.12 us: attend_tile(): jnp.einsum('qkgd,nkd->kgqn', query_halves[portion], key_sub, preferred_el...]
    ppermute x1 -> x3, waiting for transfers between devices: 4.6 us -> 0.01 us  [shifted(): lax.ppermute(shard, axis, [(i, (i + by) % peers) for i in range(peers)])]
    unnamed x30 -> x23, local copies, waits for them, and re-layouts: 6.65 us -> 10.5 us
    all_to_all x1 -> x0, starting transfers between devices: 3.81 us -> none  [on_device(): lax.all_to_all(outgoing, 'blk', split_axis=2, concat_axis=2, tiled=True)]
    ppermute x1 -> x3, starting transfers between devices: 4.04 us -> 7.09 us  [shifted(): lax.ppermute(shard, axis, [(i, (i + by) % peers) for i in range(peers)])]
    scatter x1 -> x0, local copies, waits for them, and re-layouts: 2.14 us -> none  [on_device(): cache_rows = jnp.zeros((token_rows // HEAD_DIVISIONS, 2 * KEY_VALUE_HEADS...]
  transfers between devices with their start and end apart: 2 -> 9, of which waited for: 1 -> 1; matrix products, arithmetic and copies ran while one was open for 40% -> 7% of each run, Pallas kernels for 0% -> 19%
where the time goes in v1:
time: 47.8 us; the launch traced here: 47.3 us
  starting transfers between devices  17 us (36%)
  Pallas kernels  11.4 us (24%)
  local copies, waits for them, and re-layouts  10.5 us (22%)
  blocking collectives  4.9 us (10%)
  other arithmetic  1.37 us (3%)
  between operations  1.35 us (3%)
  waiting for transfers between devices  0.83 us (2%)
    unnamed x23, local copies, waits for them, and re-layouts  10.5 us
    ppermute x6, starting transfers between devices, crossed(): return lax.ppermute(shard, axis, [(i, i ^ by) for i in range(peers)])  9.89 us
    ppermute x3, starting transfers between devices, shifted(): lax.ppermute(shard, axis, [(i, (i + by) % peers) for i in range(peers)])  7.09 us
    unnamed x1, blocking collectives  4.9 us
    pallas_call x1, Pallas kernels, other_keys(): call(body, shapes, [SMEM] * 4 + [VMEM] * (5 + slots), 'other_keys', scrat...  3.1 us
    pallas_call x1, Pallas kernels, own_part(): call(body, shapes, [SMEM, SMEM] + [VMEM] * 5, 'own_part', flops=4 * 10 **...  2.86 us
    pallas_call x1, Pallas kernels, finish(): call(body, shape, [SMEM] * 2 + [VMEM] * (2 + 3 * (slots - 1)), 'finish',...  2.34 us
    pallas_call x1, Pallas kernels, cache_part(): call(body, shape, [SMEM] * 4 + [VMEM] * 8, 'cache_part')  2.33 us
  transfers between devices with their start and end apart: 9, of which 1 were waited for; matrix products, arithmetic and copies ran while one was open for 7% of the time, Pallas kernels for 19%

profile of v1, /device:TPU:0, one launch (start us, length us, event | category | flops | bytes accessed | tf_op | source)
XLA Modules:
  0.0 47.3 jit_solution(12669019047235511411)
XLA Ops:
  0.6 4.1 %collective-permute-start = (bf16[512,256]{1,0:T(8,128)(2,1)}, bf16[512,256]{1,0:T(8,128)(2,1)S(1)}, u32[]{:S(2)}, u32[]{:S(2)}) collective-permute-start(bf16[512,256]{1,0:T(8,128)(2,1)} %bitcast.27), channel_id=1, source_target_pairs={{0,4},{1,5},{2,6},{3,7},{4,0},{5,1},{6,2},{7,3},{8,12},{9,13},{10,... | collective-permute-start | bytes 786440 | tf_op jit(solution)/shard_map/ppermute | solution.py:32
  4.7 0.0 copy-start
  4.7 0.9 %copy-done = bf16[1,1,512,256]{3,2,1,0:T(8,128)(2,1)S(1)} copy-done((bf16[1,1,512,256]{3,2,1,0:T(8,128)(2,1)S(1)}, bf16[1,1,512,256]{3,2,1,0:T(8,128)(2,1)}, u32[]{:S(2)}) %copy-start) | copy-done | bytes 262168
  5.7 0.0 copy-start.6
  5.7 0.7 %copy-done.6 = s32[1,8]{1,0:T(1,128)S(1)} copy-done((s32[1,8]{1,0:T(1,128)S(1)}, s32[1,8]{1,0:T(1,128)}, u32[]{:S(2)}) %copy-start.6) | copy-done | bytes 56
  6.3 0.8 %order_values.1 = (bf16[256,256]{1,0:T(8,128)(2,1)S(1)}, bf16[256,256]{1,0:T(8,128)(2,1)S(1)}) custom-call(s32[1]{0:T(128)} %bitcast.me_ref, s32[1,8]{1,0:T(1,128)S(1)} %copy-done.6, bf16[512,256]{1,0:T(8,128)(2,1)S(1)} %bitcast.22), custom_call_target="tpu_custom_call" | custom-call | flops 100000000 | bytes 1000000 | tf_op jit(solution)/shard_map/order_values/pallas_call | solution.py:136
  7.1 0.1 collective-permute-start.1
  7.9 1.2 %dynamic-slice = u32[1]{0:T(128)} dynamic-slice(u32[32]{0:T(128)} %constant.24, u32[]{:T(128)S(6)} %add), dynamic_slice_sizes={1} | dynamic-slice | bytes 12
  9.1 0.8 %dynamic-update-slice = s32[4]{0:T(128)S(1)} dynamic-update-slice(s32[4]{0:T(128)S(1)} %broadcast, s32[1]{0:T(128)S(6)} %copy.20, u32[]{:T(128)} %bitcast.4) | dynamic-update-slice | bytes 12
  9.9 2.9 %collective-permute-start.2 = (bf16[256,256]{1,0:T(8,128)(2,1)S(1)}, bf16[256,256]{1,0:T(8,128)(2,1)S(1)}, u32[]{:S(2)}, u32[]{:S(2)}) collective-permute-start(bf16[256,256]{1,0:T(8,128)(2,1)S(1)} %get-tuple-element.21), channel_id=1, source_target_pairs={{0,4},{1,5},{2,6},{3,7},{4,0},{5,1},{6,2},{7,3},{8,12},{9,13},{10,... | collective-permute-start | bytes 393224 | tf_op jit(solution)/shard_map/ppermute | solution.py:32
  12.8 4.9 %all-reduce = s32[4]{0:T(128)S(1)} all-reduce(s32[4]{0:T(128)S(1)} %dynamic-update-slice), channel_id=1, replica_groups=mesh['req'=4,'blk'=8] {'req'}, use_global_device_ids=true, to_apply=%add | all-reduce | flops 4 | bytes 32
  17.7 0.0 copy-start.1
  17.7 0.9 %copy-done.1 = bf16[1,1,512,256]{3,2,1,0:T(8,128)(2,1)S(1)} copy-done((bf16[1,1,512,256]{3,2,1,0:T(8,128)(2,1)S(1)}, bf16[1,1,512,256]{3,2,1,0:T(8,128)(2,1)}, u32[]{:S(2)}) %copy-start.1) | copy-done | bytes 262168
  18.6 0.0 copy-start.2
  18.6 0.9 %copy-done.2 = f32[2,256,128]{2,1,0:T(8,128)S(1)} copy-done((f32[2,256,128]{2,1,0:T(8,128)S(1)}, f32[2,256,128]{2,1,0:T(8,128)}, u32[]{:S(2)}) %copy-start.2) | copy-done | bytes 262168
  19.6 0.0 copy-start.4
  19.6 0.7 %copy-done.4 = s32[1,2,2]{2,1,0:T(2,128)S(1)} copy-done((s32[1,2,2]{2,1,0:T(2,128)S(1)}, s32[1,2,2]{2,1,0:T(2,128)}, u32[]{:S(2)}) %copy-start.4) | copy-done | bytes 40
  20.2 0.0 copy-start.5
  20.2 0.7 %copy-done.5 = f32[2,4,128]{2,1,0:T(4,128)S(1)} copy-done((f32[2,4,128]{2,1,0:T(4,128)S(1)}, f32[2,4,128]{2,1,0:T(4,128)}, u32[]{:S(2)}) %copy-start.5) | copy-done | bytes 4120
  20.9 0.0 copy-start.8
  20.9 1.0 %copy-done.8 = bf16[1,1,512,512]{3,2,1,0:T(8,128)(2,1)S(1)} copy-done((bf16[1,1,512,512]{3,2,1,0:T(8,128)(2,1)S(1)}, bf16[1,1,512,512]{3,2,1,0:T(8,128)(2,1)}, u32[]{:S(2)}) %copy-start.8) | copy-done | bytes 524312
  22.0 0.0 copy-start.9
  22.0 0.9 %copy-done.9 = bf16[1,1,512,256]{3,2,1,0:T(8,128)(2,1)S(1)} copy-done((bf16[1,1,512,256]{3,2,1,0:T(8,128)(2,1)S(1)}, bf16[1,1,512,256]{3,2,1,0:T(8,128)(2,1)}, u32[]{:S(2)}) %copy-start.9) | copy-done | bytes 262168
  22.9 2.9 %own_part.1 = (bf16[512,512]{1,0:T(8,128)(2,1)S(1)}, bf16[512,256]{1,0:T(8,128)(2,1)S(1)}, f32[512,512]{1,0:T(8,128)S(1)}, f32[512,512]{1,0:T(8,128)S(1)}) custom-call(s32[1]{0:T(128)} %bitcast.me_ref, s32[1,2,2]{2,1,0:T(2,128)S(1)} %copy-done.4, bf16[512,512]{1,0:T(8,128)(2,1)S(1)} %bitcast.26, bf16[512,256]{1,0:T(8,128)(2,1)S(1)} %bitcast.28, ...), custom_call_target="tpu_custom_call" | custom-call | flops 400000000 | bytes 4000000 | tf_op jit(solution)/shard_map/own_part/pallas_call | solution.py:186
  25.8 1.4 %fusion = s32[]{:T(128)} fusion(s32[4]{0:T(128)S(1)} %all-reduce, s32[4]{0:T(128)} %param.14, s32[]{:T(128)S(6)} %axis_index.25), kind=kLoop, calls=%fused_computation.1 | loop fusion | flops 11 | bytes 40 | tf_op jit(solution)/shard_map/reduce_sum | solution.py:371
  27.2 0.0 collective-permute-done.rest_0_
  27.2 0.0 copy-start.3
  27.2 0.9 %copy-done.3 = f32[2,256,128]{2,1,0:T(8,128)S(1)} copy-done((f32[2,256,128]{2,1,0:T(8,128)S(1)}, f32[2,256,128]{2,1,0:T(8,128)}, u32[]{:S(2)}) %copy-start.3) | copy-done | bytes 262168
  28.1 0.0 copy-start.7
  28.1 0.7 %copy-done.7 = s32[1,8]{1,0:T(1,128)S(1)} copy-done((s32[1,8]{1,0:T(1,128)S(1)}, s32[1,8]{1,0:T(1,128)}, u32[]{:S(2)}) %copy-start.7) | copy-done | bytes 56
  28.8 3.1 %other_keys.1 = (bf16[4,512,512]{2,1,0:T(8,128)(2,1)S(1)}, f32[512,128]{1,0:T(8,128)S(1)}, bf16[192,256]{1,0:T(8,128)(2,1)S(1)}, bf16[192,256]{1,0:T(8,128)(2,1)...) custom-call(s32[1]{0:T(128)} %bitcast.me_ref, s32[1,2,2]{2,1,0:T(2,128)S(1)} %copy-done.4, ...), custom_call_target="tpu_custom_call" | custom-call | flops 300000000 | bytes 4000000 | tf_op jit(solution)/shard_map/other_keys/pallas_call | solution.py:261
  31.9 1.6 %collective-permute-start.3 = (bf16[192,256]{1,0:T(8,128)(2,1)S(1)}, bf16[192,256]{1,0:T(8,128)(2,1)S(1)}, u32[]{:S(2)}, u32[]{:S(2)}) collective-permute-start(bf16[192,256]{1,0:T(8,128)(2,1)S(1)} %get-tuple-element.23), channel_id=1, source_target_pairs={{0,1},{1,0},{2,3},{3,2},{4,5},{5,4},{6,7},{7,6},{8,9},{9,8},{10,11... | collective-permute-start | bytes 294920 | tf_op jit(solution)/shard_map/ppermute | solution.py:37
  33.5 1.6 %collective-permute-start.4 = (bf16[192,256]{1,0:T(8,128)(2,1)S(1)}, bf16[192,256]{1,0:T(8,128)(2,1)S(1)}, u32[]{:S(2)}, u32[]{:S(2)}) collective-permute-start(bf16[192,256]{1,0:T(8,128)(2,1)S(1)} %get-tuple-element.24), channel_id=1, source_target_pairs={{0,2},{1,3},{2,0},{3,1},{4,6},{5,7},{6,4},{7,5},{8,10},{9,11},{10,... | collective-permute-start | bytes 294920 | tf_op jit(solution)/shard_map/ppermute | solution.py:37
  35.0 0.4 collective-permute-start.5
  35.4 0.0 collective-permute-done.1.refs_1_
  35.5 1.6 %collective-permute-start.6 = (bf16[64,256]{1,0:T(8,128)(2,1)S(1)}, bf16[64,256]{1,0:T(8,128)(2,1)S(1)}, u32[]{:S(2)}, u32[]{:S(2)}) collective-permute-start(bf16[64,256]{1,0:T(8,128)(2,1)S(1)} %bitcast.33), channel_id=1, source_target_pairs={{0,1},{1,0},{2,3},{3,2},{4,5},{5,4},{6,7},{7,6},{8,9},{9,8},{10,11... | collective-permute-start | bytes 98312 | tf_op jit(solution)/shard_map/ppermute | solution.py:37
  37.0 0.0 collective-permute-done.2.refs_2_
  37.0 1.6 %collective-permute-start.7 = (bf16[64,256]{1,0:T(8,128)(2,1)S(1)}, bf16[64,256]{1,0:T(8,128)(2,1)S(1)}, u32[]{:S(2)}, u32[]{:S(2)}) collective-permute-start(bf16[64,256]{1,0:T(8,128)(2,1)S(1)} %bitcast.32), channel_id=1, source_target_pairs={{0,2},{1,3},{2,0},{3,1},{4,6},{5,7},{6,4},{7,5},{8,10},{9,11},{10,... | collective-permute-start | bytes 98312 | tf_op jit(solution)/shard_map/ppermute | solution.py:37
  38.6 0.8 %collective-permute-done.6.refs_5_ = bf16[64,256]{1,0:T(8,128)(2,1)S(1)} collective-permute-done((bf16[64,256]{1,0:T(8,128)(2,1)S(1)}, bf16[64,256]{1,0:T(8,128)(2,1)S(1)}, u32[]{:S(2)}, u32[]{:S(2)}) %collective-permute-start.6) | collective-permute-done | bytes 32800 | tf_op jit(solution)/shard_map/ppermute | solution.py:37
  39.4 3.2 %collective-permute-start.8 = (bf16[64,256]{1,0:T(8,128)(2,1)S(1)}, bf16[64,256]{1,0:T(8,128)(2,1)S(1)}, u32[]{:S(2)}, u32[]{:S(2)}) collective-permute-start(bf16[64,256]{1,0:T(8,128)(2,1)S(1)} %bitcast.31), channel_id=1, source_target_pairs={{0,3},{1,2},{2,1},{3,0},{4,7},{5,6},{6,5},{7,4},{8,11},{9,10},{10,... | collective-permute-start | bytes 98312 | tf_op jit(solution)/shard_map/ppermute | solution.py:37
  42.6 2.3 %finish.1 = bf16[512,512]{1,0:T(8,128)(2,1)} custom-call(s32[1]{0:T(128)} %bitcast.me_ref, s32[1,2,2]{2,1,0:T(2,128)S(1)} %copy-done.4, f32[512,512]{1,0:T(8,128)S(1)} %get-tuple-element.14.num_ref, f32[512,128]{1,0:T(8,128)S(1)} %get-tuple-element.18.inv_ref, bf16[4,512,512]{2,1,0:T(8,128)(2,1)S(1)} %get-tuple-element.19.refs_0_, ...), custom_call_target="tpu_custom_call" | custom-call | flops 300000000 | bytes 4000000 | tf_op jit(solution)/shard_map/finish/pallas_call | solution.py:345
  44.9 0.0 collective-permute-done.7.refs_6_
  44.9 0.0 collective-permute-done.8.refs_7_
  45.0 0.0 collective-permute-done.3.refs_1_
  45.0 0.0 collective-permute-done.4.refs_2_
  45.0 0.0 collective-permute-done.5.refs_3_
  45.0 2.3 %cache_part.1 = bf16[128,2048]{1,0:T(8,128)(2,1)} custom-call(s32[1]{0:T(128)} %bitcast.me_ref, s32[1,2,2]{2,1,0:T(2,128)S(1)} %copy-done.4, s32[1,8]{1,0:T(1,128)S(1)} %copy-done.7, s32[1]{0:T(128)} %bitcast.5.len_ref, bf16[192,256]{1,0:T(8,128)(2,1)S(1)} %get-tuple-element.22.refs_0_, bf16[192,256]{1,0:T(8,128)(2,1)S(1)} %collective-permute-done.3.refs_1_, ...), custom_call_target="tpu_custom_call" | custom-call | flops 100000000 | bytes 1000000 | tf_op jit(solution)/shard_map/cache_part/pallas_call | solution.py:305
  (2 shorter events, 0.0 us)
Async XLA Ops:
  0.6 26.5 %collective-permute-start = (bf16[512,256]{1,0:T(8,128)(2,1)}, bf16[512,256]{1,0:T(8,128)(2,1)S(1)}, u32[]{:S(2)}, u32[]{:S(2)}) collective-permute-start(bf16[512,256]{1,0:T(8,128)(2,1)} %bitcast.27), channel_id=1, source_target_pairs={{0,4},{1,5},{2,6},{3,7},{4,0},{5,1},{6,2},{7,3},{8,12},{9,13},{10,... | collective-permute-start | bytes 786440 | tf_op jit(solution)/shard_map/ppermute | solution.py:32
  4.7 0.9 %copy-start = (bf16[1,1,512,256]{3,2,1,0:T(8,128)(2,1)S(1)}, bf16[1,1,512,256]{3,2,1,0:T(8,128)(2,1)}, u32[]{:S(2)}) copy-start(bf16[1,1,512,256]{3,2,1,0:T(8,128)(2,1)} %param.11) | copy-start | bytes 786436
  5.7 0.7 %copy-start.6 = (s32[1,8]{1,0:T(1,128)S(1)}, s32[1,8]{1,0:T(1,128)}, u32[]{:S(2)}) copy-start(s32[1,8]{1,0:T(1,128)} %rank_ref.5) | copy-start | bytes 100
  7.1 28.3 %collective-permute-start.1 = (bf16[256,256]{1,0:T(8,128)(2,1)S(1)}, bf16[256,256]{1,0:T(8,128)(2,1)S(1)}, u32[]{:S(2)}, u32[]{:S(2)}) collective-permute-start(bf16[256,256]{1,0:T(8,128)(2,1)S(1)} %get-tuple-element.20), channel_id=1, source_target_pairs={{0,4},{1,5},{2,6},{3,7},{4,0},{5,1},{6,2},{7,3},{8,12},{9,13},{10,... | collective-permute-start | bytes 393224 | tf_op jit(solution)/shard_map/ppermute | solution.py:32
  9.9 27.2 %collective-permute-start.2 = (bf16[256,256]{1,0:T(8,128)(2,1)S(1)}, bf16[256,256]{1,0:T(8,128)(2,1)S(1)}, u32[]{:S(2)}, u32[]{:S(2)}) collective-permute-start(bf16[256,256]{1,0:T(8,128)(2,1)S(1)} %get-tuple-element.21), channel_id=1, source_target_pairs={{0,4},{1,5},{2,6},{3,7},{4,0},{5,1},{6,2},{7,3},{8,12},{9,13},{10,... | collective-permute-start | bytes 393224 | tf_op jit(solution)/shard_map/ppermute | solution.py:32
  17.7 0.9 %copy-start.1 = (bf16[1,1,512,256]{3,2,1,0:T(8,128)(2,1)S(1)}, bf16[1,1,512,256]{3,2,1,0:T(8,128)(2,1)}, u32[]{:S(2)}) copy-start(bf16[1,1,512,256]{3,2,1,0:T(8,128)(2,1)} %param.11) | copy-start | bytes 786436
  18.6 0.9 %copy-start.2 = (f32[2,256,128]{2,1,0:T(8,128)S(1)}, f32[2,256,128]{2,1,0:T(8,128)}, u32[]{:S(2)}) copy-start(f32[2,256,128]{2,1,0:T(8,128)} %constant.14.clone.row_ref) | copy-start | bytes 786436
  19.6 0.7 %copy-start.4 = (s32[1,2,2]{2,1,0:T(2,128)S(1)}, s32[1,2,2]{2,1,0:T(2,128)}, u32[]{:S(2)}) copy-start(s32[1,2,2]{2,1,0:T(2,128)} %map_ref.7) | copy-start | bytes 52
  20.2 0.7 %copy-start.5 = (f32[2,4,128]{2,1,0:T(4,128)S(1)}, f32[2,4,128]{2,1,0:T(4,128)}, u32[]{:S(2)}) copy-start(f32[2,4,128]{2,1,0:T(4,128)} %constant.15.clone.blk_ref) | copy-start | bytes 12292
  20.9 1.0 %copy-start.8 = (bf16[1,1,512,512]{3,2,1,0:T(8,128)(2,1)S(1)}, bf16[1,1,512,512]{3,2,1,0:T(8,128)(2,1)}, u32[]{:S(2)}) copy-start(bf16[1,1,512,512]{3,2,1,0:T(8,128)(2,1)} %param.9) | copy-start | bytes 1572868
  22.0 0.9 %copy-start.9 = (bf16[1,1,512,256]{3,2,1,0:T(8,128)(2,1)S(1)}, bf16[1,1,512,256]{3,2,1,0:T(8,128)(2,1)}, u32[]{:S(2)}) copy-start(bf16[1,1,512,256]{3,2,1,0:T(8,128)(2,1)} %param.10) | copy-start | bytes 786436
  27.2 1.0 %copy-start.3 = (f32[2,256,128]{2,1,0:T(8,128)S(1)}, f32[2,256,128]{2,1,0:T(8,128)}, u32[]{:S(2)}) copy-start(f32[2,256,128]{2,1,0:T(8,128)} %constant.14.clone.row_ref) | copy-start | bytes 786436
  28.1 0.7 %copy-start.7 = (s32[1,8]{1,0:T(1,128)S(1)}, s32[1,8]{1,0:T(1,128)}, u32[]{:S(2)}) copy-start(s32[1,8]{1,0:T(1,128)} %rank_ref.5) | copy-start | bytes 100
  31.9 13.1 %collective-permute-start.3 = (bf16[192,256]{1,0:T(8,128)(2,1)S(1)}, bf16[192,256]{1,0:T(8,128)(2,1)S(1)}, u32[]{:S(2)}, u32[]{:S(2)}) collective-permute-start(bf16[192,256]{1,0:T(8,128)(2,1)S(1)} %get-tuple-element.23), channel_id=1, source_target_pairs={{0,1},{1,0},{2,3},{3,2},{4,5},{5,4},{6,7},{7,6},{8,9},{9,8},{10,11... | collective-permute-start | bytes 294920 | tf_op jit(solution)/shard_map/ppermute | solution.py:37
  33.5 11.5 %collective-permute-start.4 = (bf16[192,256]{1,0:T(8,128)(2,1)S(1)}, bf16[192,256]{1,0:T(8,128)(2,1)S(1)}, u32[]{:S(2)}, u32[]{:S(2)}) collective-permute-start(bf16[192,256]{1,0:T(8,128)(2,1)S(1)} %get-tuple-element.24), channel_id=1, source_target_pairs={{0,2},{1,3},{2,0},{3,1},{4,6},{5,7},{6,4},{7,5},{8,10},{9,11},{10,... | collective-permute-start | bytes 294920 | tf_op jit(solution)/shard_map/ppermute | solution.py:37
  35.0 9.9 %collective-permute-start.5 = (bf16[192,256]{1,0:T(8,128)(2,1)S(1)}, bf16[192,256]{1,0:T(8,128)(2,1)S(1)}, u32[]{:S(2)}, u32[]{:S(2)}) collective-permute-start(bf16[192,256]{1,0:T(8,128)(2,1)S(1)} %get-tuple-element.25), channel_id=1, source_target_pairs={{0,3},{1,2},{2,1},{3,0},{4,7},{5,6},{6,5},{7,4},{8,11},{9,10},{10,... | collective-permute-start | bytes 294920 | tf_op jit(solution)/shard_map/ppermute | solution.py:37
  35.5 4.0 %collective-permute-start.6 = (bf16[64,256]{1,0:T(8,128)(2,1)S(1)}, bf16[64,256]{1,0:T(8,128)(2,1)S(1)}, u32[]{:S(2)}, u32[]{:S(2)}) collective-permute-start(bf16[64,256]{1,0:T(8,128)(2,1)S(1)} %bitcast.33), channel_id=1, source_target_pairs={{0,1},{1,0},{2,3},{3,2},{4,5},{5,4},{6,7},{7,6},{8,9},{9,8},{10,11... | collective-permute-start | bytes 98312 | tf_op jit(solution)/shard_map/ppermute | solution.py:37
  37.0 7.9 %collective-permute-start.7 = (bf16[64,256]{1,0:T(8,128)(2,1)S(1)}, bf16[64,256]{1,0:T(8,128)(2,1)S(1)}, u32[]{:S(2)}, u32[]{:S(2)}) collective-permute-start(bf16[64,256]{1,0:T(8,128)(2,1)S(1)} %bitcast.32), channel_id=1, source_target_pairs={{0,2},{1,3},{2,0},{3,1},{4,6},{5,7},{6,4},{7,5},{8,10},{9,11},{10,... | collective-permute-start | bytes 98312 | tf_op jit(solution)/shard_map/ppermute | solution.py:37
  39.4 5.5 %collective-permute-start.8 = (bf16[64,256]{1,0:T(8,128)(2,1)S(1)}, bf16[64,256]{1,0:T(8,128)(2,1)S(1)}, u32[]{:S(2)}, u32[]{:S(2)}) collective-permute-start(bf16[64,256]{1,0:T(8,128)(2,1)S(1)} %bitcast.31), channel_id=1, source_target_pairs={{0,3},{1,2},{2,1},{3,0},{4,7},{5,6},{6,5},{7,4},{8,11},{9,10},{10,... | collective-permute-start | bytes 98312 | tf_op jit(solution)/shard_map/ppermute | solution.py:37
